TPU v7x, 512 devices: a whole 4x8x8 slice. The times are simulated.
512 devices in a mesh: dp: 16 (over x, z_lo, core), fsdp: 32 (over y, z_hi).
Axes of the slice: x: 4, y: 8, z: 8 (z_hi: 4, z_lo: 2; z = z_hi * 2 + z_lo), core: 2. Of those that a mesh axis runs over, the one named last changes fastest.
Arguments:
- tokens: bfloat16 [2048, 4096], P(('dp', 'fsdp')), may hold values from -6 to 6
- cotangent: bfloat16 [2048, 4096], P(('dp', 'fsdp')), may hold values from -6 to 6
- w_in: bfloat16 [1152, 128, 128], P('fsdp'), may hold values from -0.1875 to 0.1875
- w_out: bfloat16 [1152, 128, 128], P('fsdp'), may hold values from -0.09375 to 0.09375
- in_rows: int32 [1152], P('fsdp'), may hold values from -1 to 127, as said below
- in_cols: int32 [1152], P('fsdp'), may hold values from -1 to 31, as said below
- out_rows: int32 [1152], P('fsdp'), may hold values from -1 to 127, as said below
- out_cols: int32 [1152], P('fsdp'), may hold values from -1 to 31, as said below
Outputs:
- mixed: bfloat16 [2048, 4096], P(('dp', 'fsdp'))
- input_grad: bfloat16 [2048, 4096], P(('dp', 'fsdp'))
- in_grad: bfloat16 [1152, 128, 128], P('fsdp')
- out_grad: bfloat16 [1152, 128, 128], P('fsdp')
Inputs may be any that keep to these rules, and one draw needn't show every extreme that they name: `in_rows`: slot s lies on fsdp device s // 36. A live slot names a hidden panel r with r // 4 equal to that device; -1 marks an empty slot, and empty slots follow the live ones of their device. No (panel, column block) pair is named twice. On some device all 36 slots are live, on every device at least 24. `in_cols`: -1 exactly where in_rows is -1. `out_rows`: as in_rows, for w_out. `out_cols`: -1 exactly where out_rows is -1.
All inputs are finite; a program needn't handle non-finite values.
Results may differ from a plain program's by a relative error of at most 0.025.
Values may be sent and summed in bfloat16 or wider, within the bound.
A program may use at most 64 MiB of HBM per device.

v0:
```python
import jax
import jax.numpy as jnp
from jax import lax
from jax.sharding import PartitionSpec as P

FF = 16384


def gelu_slope(values):
    cdf = 0.5 * (1.0 + jax.scipy.special.erf(values * 0.7071067811865476))
    return cdf + values * jnp.exp(-0.5 * values * values) * 0.3989422804014327


def slot_tables(slot_rows, slot_cols, per_dev):
    is_live = slot_rows >= 0
    safe_panel = jnp.where(is_live, slot_rows % per_dev, 0)
    safe_column = jnp.where(is_live, slot_cols, 0)
    return (is_live, safe_panel, safe_column)


def pick_blocks(values, slot_index, group_count):
    shaped = values.reshape(values.shape[0], group_count, 128)
    return jnp.take(shaped, slot_index, axis=1)


def fold_slots(is_live, target, contrib, count):
    selector = jnp.logical_and(
        target[:, None] == jnp.arange(count, dtype=jnp.int32)[None, :], is_live[:, None]
    )
    selector = selector.astype(jnp.float32)
    summed = jnp.einsum("stf,sp->tpf", contrib, selector, precision=lax.Precision.HIGHEST)
    return summed.reshape(summed.shape[0], -1)


def local(tokens, cotangent, w_in, w_out, in_rows, in_cols, out_rows, out_cols):
    nfsdp = lax.axis_size("fsdp")
    per_dev = FF // 128 // nfsdp
    width = tokens.shape[1]
    ncol = width // 128
    in_live, in_panel, in_column = slot_tables(in_rows, in_cols, per_dev)
    out_live, out_panel, out_column = slot_tables(out_rows, out_cols, per_dev)
    gathered = lax.all_gather(tokens, "fsdp", axis=0, tiled=True)
    x_pick = pick_blocks(gathered, in_column, ncol)
    pre_act = fold_slots(
        in_live,
        in_panel,
        jnp.einsum("tsd,sfd->stf", x_pick, w_in, preferred_element_type=jnp.float32),
        per_dev,
    )
    hidden = jax.nn.gelu(pre_act, approximate=False).astype(jnp.bfloat16)
    h_pick = pick_blocks(hidden, out_panel, per_dev)
    row_part = h_pick
    contrib = jnp.einsum("tsf,sfd->std", row_part, w_out, preferred_element_type=jnp.float32)
    mixed = lax.psum_scatter(
        fold_slots(out_live, out_column, contrib, ncol).astype(jnp.bfloat16),
        "fsdp",
        scatter_dimension=0,
        tiled=True,
    )
    cot_rows = lax.all_gather(cotangent, "fsdp", axis=0, tiled=True)
    c_pick = pick_blocks(cot_rows, out_column, ncol)
    d_hidden = fold_slots(
        out_live,
        out_panel,
        jnp.einsum("tsd,sfd->stf", c_pick, w_out, preferred_element_type=jnp.float32),
        per_dev,
    )
    d_pre = (d_hidden * gelu_slope(pre_act)).astype(jnp.bfloat16)
    d_pick = pick_blocks(d_pre, in_panel, per_dev)
    grad_out = jnp.einsum("tsf,tsd->sfd", h_pick, c_pick, preferred_element_type=jnp.float32)
    grad_out = jnp.where(out_live[:, None, None], grad_out, 0.0)
    row_part = d_pick
    contrib = jnp.einsum("tsf,sfd->std", row_part, w_in, preferred_element_type=jnp.float32)
    input_grad = lax.psum_scatter(
        fold_slots(in_live, in_column, contrib, ncol).astype(jnp.bfloat16),
        "fsdp",
        scatter_dimension=0,
        tiled=True,
    )
    grad_in = jnp.einsum("tsf,tsd->sfd", d_pick, x_pick, preferred_element_type=jnp.float32)
    grad_in = jnp.where(in_live[:, None, None], grad_in, 0.0)
    out_total, in_total = (
        lax.psum(grad_out.astype(jnp.bfloat16), "dp").astype(jnp.float32),
        lax.psum(grad_in.astype(jnp.bfloat16), "dp").astype(jnp.float32),
    )
    return (mixed, input_grad, in_total.astype(jnp.bfloat16), out_total.astype(jnp.bfloat16))


def solution(mesh):
    placed = (
        P(("dp", "fsdp"), None),
        P(("dp", "fsdp"), None),
        P("fsdp", None, None),
        P("fsdp", None, None),
        P("fsdp"),
        P("fsdp"),
        P("fsdp"),
        P("fsdp"),
    )
    return jax.shard_map(
        local,
        mesh=mesh,
        in_specs=placed,
        out_specs=(
            P(("dp", "fsdp"), None),
            P(("dp", "fsdp"), None),
            P("fsdp", None, None),
            P("fsdp", None, None),
        ),
        check_vma=False,
    )
```

profile of v0, /device:TPU:1, one launch (start us, length us, event | category | flops | bytes accessed | tf_op | source)
XLA Modules:
  0.0 687.1 jit_solution(2108964944030363270)
XLA Ops:
  7.2 0.0 copy-start
  7.2 0.0 all-gather.5.cloned.1.call-start
  7.2 0.7 all-gather.5.cloned.1.call-update
  7.9 0.0 all-gather.7.cloned.1.call-start
  8.0 0.7 all-gather.7.cloned.1.call-update
  8.7 0.0 all-reduce.7.cloned.1.call-start
  8.7 0.7 compare_and_fusion
  9.4 0.7 compare_and_fusion.1
  10.1 0.0 copy-start.5
  10.1 0.0 copy-start.7
  10.2 86.8 %all-gather.5.cloned.1.call-done = bf16[32,4,4096]{2,1,0:T(4,128)(2,1)} async-done(((bf16[1,4,4096]{2,1,0:T(4,128)(2,1)}), bf16[32,4,4096]{2,1,0:T(4,128)(2,1)}) %all-gather.5.cloned.1.call-update) | async-done | bytes 1048592 | tf_op jit(solution)/shard_map/all_gather | solution.py:42
  97.0 2.1 reshape.40
  99.2 0.4 copy.38
  99.6 81.3 %all-gather.7.cloned.1.call-done = bf16[32,4,4096]{2,1,0:T(4,128)(2,1)} async-done(((bf16[1,4,4096]{2,1,0:T(4,128)(2,1)}), bf16[32,4,4096]{2,1,0:T(4,128)(2,1)}) %all-gather.7.cloned.1.call-update) | async-done | bytes 1048592 | tf_op jit(solution)/shard_map/all_gather | solution.py:60
  180.9 2.9 reshape.41
  183.8 1.6 copy.42
  185.5 1.8 gather_fusion
  187.3 0.0 copy-done
  187.3 2.2 fusion.24
  189.5 3.0 fusion.6
  192.5 0.8 gather_fusion.2
  193.3 0.0 copy-done.5
  193.3 2.3 fusion.18
  195.5 0.0 copy-start.4
  195.5 2.3 fusion.2
  197.8 0.0 copy-done.4
  197.8 0.7 fusion.34
  198.5 1.8 gather_fusion.3
  200.3 1.8 fusion.15
  202.1 2.8 fusion.11
  204.9 1.4 copy.69
  206.3 1.8 gather_fusion.1
  208.1 0.0 copy-done.7
  208.1 2.3 fusion.21
  210.5 2.8 fusion.8
  213.2 1.5 copy.70
  214.7 0.0 copy-start.1
  214.7 0.0 all-reduce.7.cloned.1.call-update
  214.7 0.0 all-reduce.9.cloned.1.call-start
  214.8 1.2 copy-done.1
  216.0 0.0 copy-start.2
  216.0 0.0 copy-start.6
  216.0 0.0 copy-start.8
  216.0 3.2 select_convert_fusion.1
  219.1 0.0 copy-done.2
  219.1 0.0 copy-done.6
  219.1 0.0 copy-done.8
  219.1 1.8 select_convert_fusion
  221.0 0.0 all-reduce.9.cloned.1.call-update
  221.0 1.3 dynamic-slice
  222.9 298.3 %all-reduce.7.cloned.1.call-done = (bf16[128,4096]{1,0:T(8,128)(2,1)}, bf16[128,4096]{1,0:T(8,128)(2,1)}) async-done(((bf16[128,4096]{1,0:T(8,128)(2,1)}, bf16[128,4096]{1,0:T(8,128)(2,1)}), (bf16[128,4096]{1,0:T(8,128)(2,1)}, bf16[128,4096]{1,0:T(8,128)(2,1)})) %all-reduce.7.cloned.1.call-update) | async-done | bytes 2097168
  521.2 1.5 constant_dynamic-slice_fusion
  522.8 154.3 %all-reduce.9.cloned.1.call-done = (bf16[36,128,128]{2,1,0:T(8,128)(2,1)}, bf16[36,128,128]{2,1,0:T(8,128)(2,1)}) async-done(((bf16[36,128,128]{2,1,0:T(8,128)(2,1)}, bf16[36,128,128]{2,1,0:T(8,128)(2,1)}), (bf16[36,128,128]{2,1,0:T(8,128)(2,1)}, bf16[36,128,128]{2,1,0:T(8,128)(2,1)})) %all-reduce.9.cloned.1.call-update) | async-done | bytes 2359312 | tf_op jit(solution)/shard_map/psum | solution.py:84
  677.0 0.0 copy-start.3
  677.0 2.5 copy.75
  679.5 0.0 copy-done.3
  679.5 1.0 copy.76
  (8 shorter events, 0.0 us)
Async XLA Ops:
  7.2 180.1 %copy-start = (bf16[36,128,128]{2,1,0:T(8,128)(2,1)S(1)}, bf16[36,128,128]{2,1,0:T(8,128)(2,1)}, u32[]{:S(2)}) copy-start(bf16[36,128,128]{2,1,0:T(8,128)(2,1)} %param.14) | copy-start | bytes 3538948
  7.2 89.9 %all-gather.5.cloned.1.call-start = ((), (), s32[]{:S(2)}) async-start(), calls=%async_computation | async-start | bytes 1081344 | tf_op jit(solution)/shard_map/all_gather | solution.py:42
  7.9 173.0 %all-gather.7.cloned.1.call-start = ((), (), s32[]{:S(2)}) async-start(), calls=%async_computation.1 | async-start | bytes 1081344 | tf_op jit(solution)/shard_map/all_gather | solution.py:60
  8.7 512.6 %all-reduce.7.cloned.1.call-start = ((), (), s32[]{:S(2)}) async-start(), calls=%async_computation.2 | async-start | bytes 4194304
  10.1 183.1 %copy-start.5 = (pred[36]{0:T(512)(128)(4,1)}, pred[36]{0:T(512)(128)(4,1)S(1)}, u32[]{:S(2)}) copy-start(pred[36]{0:T(512)(128)(4,1)S(1)} %get-tuple-element.12) | copy-start | bytes 112
  10.1 198.0 %copy-start.7 = (pred[36]{0:T(512)(128)(4,1)}, pred[36]{0:T(512)(128)(4,1)S(1)}, u32[]{:S(2)}) copy-start(pred[36]{0:T(512)(128)(4,1)S(1)} %get-tuple-element.21) | copy-start | bytes 112
  195.5 2.3 copy-start.4
  214.7 1.3 copy-start.1
  214.7 462.3 %all-reduce.9.cloned.1.call-start = ((), (), s32[]{:S(2)}) async-start(), calls=%async_computation.3 | async-start | bytes 4718592 | tf_op jit(solution)/shard_map/psum | solution.py:84
  216.0 3.2 copy-start.2
  216.0 3.2 copy-start.6
  216.0 3.2 copy-start.8
  677.0 2.5 copy-start.3
Sparse Core Ops, SparseCore 0:
  11.2 85.8 all-gather.4
  100.2 80.6 all-gather.6
  214.9 306.3 all-reduce.6
  524.9 152.0 all-reduce.8
where the time goes:
time: 688 us; the launch traced here: 687 us
  waiting for transfers between devices  622 us (90%)
  matrix products  24.3 us (4%)
  local copies, waits for them, and re-layouts  23.8 us (3%)
  between operations  14.6 us (2%)
    unnamed x5, waiting for transfers between devices  300 us
    psum x1, waiting for transfers between devices, local(): lax.psum(grad_in.astype(jnp.bfloat16), 'dp').astype(jnp.float32)  154 us
    all_gather x1, waiting for transfers between devices, local(): gathered = lax.all_gather(tokens, 'fsdp', axis=0, tiled=True)  86.8 us
    all_gather x1, waiting for transfers between devices, local(): cot_rows = lax.all_gather(cotangent, 'fsdp', axis=0, tiled=True)  81.3 us
  transfers between devices with their start and end apart: 4, of which 4 were waited for; matrix products, arithmetic and copies ran while one was open for 2% of the time, Pallas kernels for 0%

commit v1 on v0

v1 whole, which is shorter than its diff:
```python
import jax
import jax.numpy as jnp
from jax import lax
from jax.experimental import pallas as pl
from jax.experimental.pallas import tpu as pltpu
from jax.sharding import PartitionSpec as P

MESH = pl.DeviceIdType.MESH
F32 = jnp.float32
BF16 = jnp.bfloat16

NY, NZ = 8, 4
CAP = 36
NCOL = 32
NPAN = 4
D = 4096
SEMS = 96


def mo(v, m=16):
    return pl.multiple_of(v, m)


def kernel(
    tok, cot, w_in, w_out, tab,
    mixed_o, igrad_o, ing_o, outg_o,
    x, zb, t1, t2, ws, wd, xb, hd, prt, rland, lland, zs, zl, g, fo, lc, l1, l2, l3,
    ssem, rsem, lsem,
):
    dp, fs = lax.axis_index("dp"), lax.axis_index("fsdp")
    y, zh = fs // NZ, fs % NZ
    px, zlo, core = dp // 4, (dp // 2) % 2, dp % 2

    def dev(d=dp, f=fs):
        return (d, f)

    z_peers = [(zh + d) % NZ for d in (1, 2, 3)]
    z_devs = [dev(f=y * NZ + j) for j in z_peers]
    right = dev(f=((y + 1) % NY) * NZ + zh)
    left = dev(f=((y + NY - 1) % NY) * NZ + zh)
    core_dev = dev(d=dp + 1 - 2 * core)
    xpa = px + 1 - 2 * (px % 2)
    xpb = (px + 2 * (px % 2) + 3) % 4
    xa_dev = dev(d=xpa * 4 + dp % 4)
    xb_dev = dev(d=xpb * 4 + dp % 4)
    zlo_dev = dev(d=dp + 2 - 4 * zlo)
    everyone = [*z_devs, right, left, core_dev, xa_dev, xb_dev, zlo_dev]

    used = [0]
    started = []

    def send(src, dst, to):
        i = used[0]
        used[0] += 1
        c = pltpu.make_async_remote_copy(
            src, dst, ssem.at[i], rsem.at[i], device_id=to, device_id_type=MESH
        )
        c.start()
        started.append(c)
        return c

    weights = [
        pltpu.make_async_copy(w, ws.at[a, pl.ds(0, CAP)], lsem.at[a])
        for a, w in enumerate((w_in, w_out))
    ]
    for c in weights:
        c.start()

    barrier = pltpu.get_barrier_semaphore()
    for to in everyone:
        pl.semaphore_signal(barrier, inc=1, device_id=to, device_id_type=MESH)

    for a, src in enumerate((tok, cot)):
        rows = src[...].astype(F32)
        for k in range(4):
            t1[a, 4 * k : 4 * k + 4, :] = rows[:, 1024 * k : 1024 * (k + 1)]
        zb[a, zh] = t1[a].astype(BF16)
    ws[0, CAP] = jnp.zeros((128, 128), BF16)
    ws[1, CAP] = jnp.zeros((128, 128), BF16)
    hd[0, NPAN] = jnp.zeros((128, 128), BF16)
    hd[1, NPAN] = jnp.zeros((128, 128), BF16)

    pl.semaphore_wait(barrier, len(everyone))

    zsend = [[send(zb.at[a, zh], zb.at[a, zh], to) for to in z_devs] for a in range(2)]

    def unfold(a):
        for j in range(NZ):
            t1[a] = zb[a, j].astype(F32)
            for k in range(4):
                t2[a, 4 * j : 4 * j + 4, 1024 * k : 1024 * (k + 1)] = t1[a, 4 * k : 4 * k + 4, :]
        x[a, y] = t2[a].astype(BF16)

    rights, lefts = (4, 3), (3, 4)
    chain_r, chain_l = [[], []], [[], []]

    def hop(a, k):
        if k < rights[a]:
            if k:
                chain_r[a][k - 1].wait_recv()
            b = (y + NY - k) % NY
            chain_r[a].append(send(x.at[a, b], x.at[a, b], right))
        if k < lefts[a]:
            if k:
                chain_l[a][k - 1].wait_recv()
            b = (y + k) % NY
            chain_l[a].append(send(x.at[a, b], x.at[a, b], left))

    def dense(a):
        if a == 0:
            for w in weights:
                w.wait()

        def one(c, _):
            for p in range(NPAN):
                slot = tab[a, p * NCOL + c]
                wd[a, pl.ds(p * 128, 128), pl.ds(mo(c * 128, 128), 128)] = ws[a, slot]
            return 0

        lax.fori_loop(0, NCOL, one, 0)

    for a in range(2):
        for c in zsend[a]:
            c.wait_recv()
        unfold(a)
        hop(a, 0)
    dense(0)
    hop(0, 1)
    hop(1, 1)
    dense(1)
    for k in (2, 3):
        hop(0, k)
        hop(1, k)
    for a in range(2):
        chain_r[a][-1].wait_recv()
        chain_l[a][-1].wait_recv()

    nt = (((1,), (1,)), ((), ()))

    def by_panel(a):
        return lax.dot_general(wd[a], x[a].reshape(128, D), nt, preferred_element_type=F32)

    def blocks(a):
        def one(c, _):
            xb[a, c] = x[a, :, :, pl.ds(mo(c * 128, 128), 128)].reshape(128, 128)
            return 0

        lax.fori_loop(0, NCOL, one, 0)

    def grads(dst, a, t, side):
        def one(s, _):
            panel = tab[t, 128 + s]
            col = tab[t, 128 + CAP + s]
            blk = jnp.dot(hd[side, panel], xb[a, col], preferred_element_type=F32)
            g[dst, pl.ds(mo(s * 128, 128), 128), :] = blk.astype(BF16)
            return 0

        lax.fori_loop(0, CAP, one, 0, unroll=4)

    def partial(dst, side, a):
        acts = hd[side, :NPAN].reshape(512, 128).astype(F32).T.astype(BF16)

        def one(n, _):
            cols = pl.ds(mo(n * 512, 512), 512)
            part = jnp.dot(acts, wd[a, :, cols], preferred_element_type=F32)
            prt[dst, :, :, cols] = part.astype(BF16).reshape(NY, 16, 512)
            return 0

        lax.fori_loop(0, D // 512, one, 0)

    def scatter(a):
        nr, nl = rights[a], lefts[a]
        rc = [send(prt.at[a, (y + nr) % NY], rland.at[a, 0], right)]
        lc_ = [send(prt.at[a, (y + NY - nl) % NY], lland.at[a, 0], left)]
        for k in range(1, 4):
            for chain, land, n, to, sign in (
                (rc, rland, nr, right, 1),
                (lc_, lland, nl, left, NY - 1),
            ):
                if k >= n:
                    continue
                yield
                chain[k - 1].wait_recv()
                own = prt[a, (y + sign * (n - k)) % NY].astype(F32)
                land[a, k - 1] = (own + land[a, k - 1].astype(F32)).astype(BF16)
                chain.append(send(land.at[a, k - 1], land.at[a, k], to))
        yield
        rc[-1].wait_recv()
        lc_[-1].wait_recv()
        t2[a] = (
            prt[a, y].astype(F32)
            + rland[a, nr - 1].astype(F32)
            + lland[a, nl - 1].astype(F32)
        )
        for j in range(NZ):
            for k in range(4):
                t1[a, 4 * k : 4 * k + 4, :] = t2[a, 4 * j : 4 * j + 4, 1024 * k : 1024 * (k + 1)]
            zs[a, j] = t1[a].astype(BF16)
        out = [send(zs.at[a, j], zl.at[a, zh], to) for j, to in zip(z_peers, z_devs)]
        yield
        for c in out:
            c.wait_recv()
        total = zs[a, zh].astype(F32)
        for j in z_peers:
            total = total + zl[a, j].astype(F32)
        t1[a] = total
        dst = (mixed_o, igrad_o)[a]
        for k in range(4):
            dst[:, 1024 * k : 1024 * (k + 1)] = t1[a, 4 * k : 4 * k + 4, :].astype(BF16)

    ha1, ha2 = ((px + 1) // 2) % 2, px // 2
    hb1, hb2 = px // 2, px % 2
    base = core * 2304
    other = 2304 - base
    ra1 = base + ha1 * 576
    sa1 = base + 576 - ha1 * 576
    ra2 = ra1 + ha2 * 288
    sa2 = ra1 + 288 - ha2 * 288
    rb1 = base + 1152 + hb1 * 576
    sb1 = base + 1152 + 576 - hb1 * 576
    rb2 = rb1 + hb2 * 288
    sb2 = rb1 + 288 - hb2 * 288
    rk = ra2 + zlo * (rb2 - ra2)
    rs = rb2 + zlo * (ra2 - rb2)

    def rows(ref, a, r, n):
        return ref.at[a, pl.ds(mo(r), n)]

    def add(a, r, n, land, step):
        def one(i, _):
            at = pl.ds(mo(r + i * step), step)
            g[a, at] = (g[a, at].astype(F32) + land[pl.ds(mo(i * step), step)].astype(F32)).astype(BF16)
            return 0

        lax.fori_loop(0, n // step, one, 0)

    def reduce(a):
        c0 = send(rows(g, a, other, 2304), lc.at[a], core_dev)
        yield
        c0.wait_recv()
        add(a, base, 2304, lc.at[a], 288)
        c1 = send(rows(g, a, sa1, 576), l1.at[a, 0], xa_dev)
        c2 = send(rows(g, a, sb1, 576), l1.at[a, 1], xb_dev)
        yield
        c1.wait_recv()
        add(a, ra1, 576, l1.at[a, 0], 288)
        c3 = send(rows(g, a, sa2, 288), l2.at[a, 0], xb_dev)
        c2.wait_recv()
        add(a, rb1, 576, l1.at[a, 1], 288)
        c4 = send(rows(g, a, sb2, 288), l2.at[a, 1], xa_dev)
        yield
        c3.wait_recv()
        add(a, ra2, 288, l2.at[a, 0], 288)
        c4.wait_recv()
        add(a, rb2, 288, l2.at[a, 1], 288)
        c5 = send(rows(g, a, rs, 288), l3.at[a], zlo_dev)
        yield
        c5.wait_recv()
        fo[a, pl.ds(mo(rk), 288)] = (
            g[a, pl.ds(mo(rk), 288)].astype(F32) + l3[a].astype(F32)
        ).astype(BF16)
        c6 = send(rows(fo, a, rk, 288), rows(fo, a, rk, 288), zlo_dev)
        yield
        c6.wait_recv()
        c7 = send(rows(fo, a, ra2, 288), rows(fo, a, ra2, 288), xb_dev)
        c8 = send(rows(fo, a, rb2, 288), rows(fo, a, rb2, 288), xa_dev)
        yield
        c7.wait_recv()
        c9 = send(rows(fo, a, ra1, 576), rows(fo, a, ra1, 576), xa_dev)
        c8.wait_recv()
        c10 = send(rows(fo, a, rb1, 576), rows(fo, a, rb1, 576), xb_dev)
        yield
        c9.wait_recv()
        c10.wait_recv()
        c11 = send(rows(fo, a, base, 2304), rows(fo, a, base, 2304), core_dev)
        yield
        c11.wait_recv()
        out = pltpu.make_async_copy(fo.at[a], (outg_o, ing_o)[a], lsem.at[3 + a])
        out.start()
        yield
        out.wait()

    def step(task):
        next(task, None)

    pre = by_panel(0)
    cdf = 0.5 * (1.0 + lax.erf(pre * 0.7071067811865476))
    hd[0, :NPAN] = (pre * cdf).astype(BF16).reshape(NPAN, 128, 128)
    slope = cdf + pre * jnp.exp(-0.5 * pre * pre) * 0.3989422804014327
    d_pre = lax.dot_general(
        wd[1], x[1].reshape(128, D), nt, preferred_element_type=F32
    )
    hd[1, :NPAN] = (d_pre * slope).astype(BF16).reshape(NPAN, 128, 128)

    blocks(1)
    grads(0, 1, 1, 0)
    red0, red1 = reduce(0), reduce(1)
    step(red0)
    blocks(0)
    grads(1, 0, 0, 1)
    step(red0)
    step(red1)
    partial(0, 0, 1)
    sc0, sc1 = scatter(0), scatter(1)
    step(sc0)
    step(red0)
    step(red1)
    partial(1, 1, 0)
    step(sc1)
    tasks = [red0, sc0, red1, sc1]
    while tasks:
        for task in list(tasks):
            if next(task, tasks) is tasks:
                tasks.remove(task)
    for c in started:
        c.wait_send()


def slot_table(in_rows, in_cols, out_rows, out_cols):
    rows, cols = jnp.stack([in_rows, out_rows]), jnp.stack([in_cols, out_cols])
    live = rows >= 0
    panel = jnp.where(live, rows % NPAN, NPAN)
    col = jnp.where(live, cols, 0)
    pair = jnp.arange(NPAN * NCOL, dtype=jnp.int32)
    slot = jnp.arange(CAP, dtype=jnp.int32)
    hit = (panel * NCOL + col)[:, :, None] == pair[None, None, :]
    where = jnp.min(jnp.where(hit, slot[None, :, None], CAP), axis=1)
    return jnp.concatenate([where, panel, col], axis=1)


def local(tokens, cotangent, w_in, w_out, in_rows, in_cols, out_rows, out_cols):
    vmem = pl.BlockSpec(memory_space=pltpu.VMEM)
    smem = pl.BlockSpec(memory_space=pltpu.SMEM)
    hbm = pl.BlockSpec(memory_space=pl.ANY)
    rows = tokens.shape[0]
    mixed, igrad, ing, outg = pl.pallas_call(
        kernel,
        out_shape=(
            jax.ShapeDtypeStruct((rows, D), BF16),
            jax.ShapeDtypeStruct((rows, D), BF16),
            jax.ShapeDtypeStruct((CAP * 128, 128), BF16),
            jax.ShapeDtypeStruct((CAP * 128, 128), BF16),
        ),
        in_specs=[vmem, vmem, hbm, hbm, smem],
        out_specs=(vmem, vmem, hbm, hbm),
        scratch_shapes=[
            pltpu.VMEM((2, NY, 16, D), BF16),
            pltpu.VMEM((2, NZ, 16, 1024), BF16),
            pltpu.VMEM((2, 16, 1024), F32),
            pltpu.VMEM((2, 16, D), F32),
            pltpu.VMEM((2, CAP + 1, 128, 128), BF16),
            pltpu.VMEM((2, 512, D), BF16),
            pltpu.VMEM((2, NCOL, 128, 128), BF16),
            pltpu.VMEM((2, NPAN + 1, 128, 128), BF16),
            pltpu.VMEM((2, NY, 16, D), BF16),
            pltpu.VMEM((2, 4, 16, D), BF16),
            pltpu.VMEM((2, 4, 16, D), BF16),
            pltpu.VMEM((2, NZ, 16, 1024), BF16),
            pltpu.VMEM((2, NZ, 16, 1024), BF16),
            pltpu.VMEM((2, 4608, 128), BF16),
            pltpu.VMEM((2, 4608, 128), BF16),
            pltpu.VMEM((2, 2304, 128), BF16),
            pltpu.VMEM((2, 2, 576, 128), BF16),
            pltpu.VMEM((2, 2, 288, 128), BF16),
            pltpu.VMEM((2, 288, 128), BF16),
            pltpu.SemaphoreType.DMA((SEMS,)),
            pltpu.SemaphoreType.DMA((SEMS,)),
            pltpu.SemaphoreType.DMA((5,)),
        ],
        compiler_params=pltpu.CompilerParams(
            collective_id=0, has_side_effects=True, vmem_limit_bytes=56 * 2**20
        ),
    )(tokens, cotangent, w_in, w_out, slot_table(in_rows, in_cols, out_rows, out_cols))
    return mixed, igrad, ing.reshape(CAP, 128, 128), outg.reshape(CAP, 128, 128)


def solution(mesh):
    placed = (
        P(("dp", "fsdp"), None),
        P(("dp", "fsdp"), None),
        P("fsdp", None, None),
        P("fsdp", None, None),
        P("fsdp"),
        P("fsdp"),
        P("fsdp"),
        P("fsdp"),
    )
    return jax.shard_map(
        local,
        mesh=mesh,
        in_specs=placed,
        out_specs=(
            P(("dp", "fsdp"), None),
            P(("dp", "fsdp"), None),
            P("fsdp", None, None),
            P("fsdp", None, None),
        ),
        check_vma=False,
    )
```

time: 688 us -> 102 us (0.15)
  the two profiles are of different devices: /device:TPU:1 before, /device:TPU:24 now
where the time goes in v1:
time: 102 us
  Pallas kernels  93 us (91%)
  local copies, waits for them, and re-layouts  6.39 us (6%)
  other arithmetic  1.49 us (1%)
    pallas_call x1, Pallas kernels, local(): pl.pallas_call(kernel, out_shape=(jax.ShapeDtypeStruct((rows, D), BF16),...  93 us
    unnamed x6, local copies, waits for them, and re-layouts  6.29 us

profile of v1, /device:TPU:24, one launch (start us, length us, event | category | flops | bytes accessed | tf_op | source)
XLA Modules:
  0.0 101.6 jit_solution(7938426331999123877)
XLA Ops:
  0.6 0.7 multiply_add_fusion
  1.4 0.1 copy.12
  1.5 0.1 fusion
  1.6 0.7 pad_add_fusion.tab
  2.2 93.0 %shard_map.111 = (bf16[4,4096]{1,0:T(4,128)(2,1)}, bf16[4,4096]{1,0:T(4,128)(2,1)}, bf16[4608,128]{1,0:T(8,128)(2,1)}, bf16[4608,128]{1,0:T(8,128)(2,1)}) custom-call(bf16[4,4096]{1,0:T(4,128)(2,1)} %tok.1, bf16[4,4096]{1,0:T(4,128)(2,1)} %cot.1, bf16[36,128,128]{2,1,0:T(8,128)(2,1)} %w_in.1, bf16[36,128,128]{2,1,0:T(8,128)(2,1)} %w_out.1, ...), custom_call_target="tpu_custom_call" | custom-call | tf_op jit(solution)/shard_map/pallas_call | solution.py:336
  95.3 1.4 %copy.17 = bf16[4,4096]{1,0:T(4,128)(2,1)} copy(bf16[4,4096]{1,0:T(4,128)(2,1)} %get-tuple-element.19) | data formatting | bytes 65536
  96.7 1.4 %copy.18 = bf16[4,4096]{1,0:T(4,128)(2,1)} copy(bf16[4,4096]{1,0:T(4,128)(2,1)} %get-tuple-element.20) | data formatting | bytes 65536
  98.0 0.0 copy-start
  98.0 2.5 %copy.19 = bf16[36,128,128]{2,1,0:T(8,128)(2,1)} copy(bf16[36,128,128]{2,1,0:T(8,128)(2,1)} %bitcast.7) | data formatting | bytes 2359296
  100.6 0.0 copy-done
  100.6 1.0 copy.20
Async XLA Ops:
  98.0 2.5 %copy-start = (bf16[4608,128]{1,0:T(8,128)(2,1)S(1)}, bf16[4608,128]{1,0:T(8,128)(2,1)}, u32[]{:S(2)}) copy-start(bf16[4608,128]{1,0:T(8,128)(2,1)} %get-tuple-element.11) | copy-start | bytes 3538948

commit v2 on v1

v2 whole, which is shorter than its diff:
```python
import jax
import jax.numpy as jnp
from jax import lax
from jax.experimental import pallas as pl
from jax.experimental.pallas import tpu as pltpu
from jax.sharding import PartitionSpec as P

MESH = pl.DeviceIdType.MESH
F32 = jnp.float32
BF16 = jnp.bfloat16

NY, NZ = 8, 4
CAP = 36
NCOL = 32
NPAN = 4
D = 4096
SEMS = 128


def mo(v, m=16):
    return pl.multiple_of(v, m)


def kernel(
    tok, cot, w_in, w_out, pair_slot, slot_pair,
    mixed_o, igrad_o, ing_o, outg_o,
    own, xg, x, t1, t2, ws, wd, xb, hd, prt, rland, lland, zs, zl, g, lc, l1, l2, l3,
    ssem, rsem, lsem,
):
    dp, fs = lax.axis_index("dp"), lax.axis_index("fsdp")
    y, zh = fs // NZ, fs % NZ
    px, zlo, core = dp // 4, (dp // 2) % 2, dp % 2

    def dev(d=dp, f=fs):
        return (d, f)

    z_peers = [(zh + d) % NZ for d in (1, 2, 3)]
    z_devs = [dev(f=y * NZ + j) for j in z_peers]
    right = dev(f=((y + 1) % NY) * NZ + zh)
    left = dev(f=((y + NY - 1) % NY) * NZ + zh)
    core_dev = dev(d=dp + 1 - 2 * core)
    xpa = px + 1 - 2 * (px % 2)
    xpb = (px + 2 * (px % 2) + 3) % 4
    xa_dev = dev(d=xpa * 4 + dp % 4)
    xb_dev = dev(d=xpb * 4 + dp % 4)
    zlo_dev = dev(d=dp + 2 - 4 * zlo)
    everyone = [*z_devs, right, left, core_dev, xa_dev, xb_dev, zlo_dev]

    used = [0]
    started = []

    def send(src, dst, to):
        i = used[0]
        used[0] += 1
        c = pltpu.make_async_remote_copy(
            src, dst, ssem.at[i], rsem.at[i], device_id=to, device_id_type=MESH
        )
        c.start()
        started.append(c)
        return c

    barrier = pltpu.get_barrier_semaphore()
    for to in everyone:
        pl.semaphore_signal(barrier, inc=1, device_id=to, device_id_type=MESH)

    fetch = [
        pltpu.make_async_copy(src, own.at[a], lsem.at[2 + a])
        for a, src in enumerate((tok, cot))
    ]
    weights = [
        pltpu.make_async_copy(w, ws.at[a, pl.ds(0, CAP)], lsem.at[a])
        for a, w in enumerate((w_in, w_out))
    ]
    for c in fetch + weights:
        c.start()

    for a in range(2):
        fetch[a].wait()
        for k in range(4):
            t1[a, 4 * k : 4 * k + 4, :] = own[a, :, 1024 * k : 1024 * (k + 1)].astype(F32)
        xg[a, y, 0] = t1[a].astype(BF16)

    pl.semaphore_wait(barrier, len(everyone))

    zsend = [
        [send(xg.at[a, y, 0], xg.at[a, y, NZ - d], to) for d, to in zip((1, 2, 3), z_devs)]
        for a in range(2)
    ]
    for a in range(2):
        ws[a, CAP] = jnp.zeros((128, 128), BF16)
        hd[a, NPAN] = jnp.zeros((128, 128), BF16)

    def unfold(a, b):
        for d in range(NZ):
            t1[a] = xg[a, b, d].astype(F32)
            for k in range(4):
                t2[a, 4 * d : 4 * d + 4, 1024 * k : 1024 * (k + 1)] = t1[a, 4 * k : 4 * k + 4, :]
        x[a, b] = t2[a].astype(BF16)

    rights, lefts = (4, 3), (3, 4)
    chains = {}

    def hop(a, grp, k):
        part = (pl.ds(0, 1), pl.ds(1, 3))[grp]
        for way, to, n, back in (
            (0, right, rights[a ^ grp], NY - 1),
            (1, left, lefts[a ^ grp], 1),
        ):
            chain = chains.setdefault((a, grp, way), [])
            if k < n:
                if k:
                    chain[k - 1].wait_recv()
                ref = xg.at[a, (y + back * k) % NY, part]
                chain.append(send(ref, ref, to))

    def arrive(a, k):
        for grp in range(2):
            for way in range(2):
                chain = chains[(a, grp, way)]
                if k == len(chain):
                    chain[k - 1].wait_recv()
        unfold(a, (y + NY - k) % NY)
        if 2 * k != NY and k:
            unfold(a, (y + k) % NY)

    def dense(a):
        if a == 0:
            for w in weights:
                w.wait()

        def one(c, _):
            for p in range(NPAN):
                slot = pair_slot[a, p * NCOL + c]
                wd[a, pl.ds(p * 128, 128), pl.ds(mo(c * 128, 128), 128)] = ws[a, slot]
            return 0

        lax.fori_loop(0, NCOL, one, 0)

    hop(0, 0, 0)
    hop(1, 0, 0)
    hop(0, 0, 1)
    hop(1, 0, 1)
    for a in range(2):
        for c in zsend[a]:
            c.wait_recv()
        hop(a, 1, 0)
    hop(0, 0, 2)
    hop(1, 0, 2)
    dense(0)
    hop(0, 1, 1)
    hop(1, 1, 1)
    hop(0, 0, 3)
    hop(1, 0, 3)
    dense(1)
    hop(0, 1, 2)
    hop(1, 1, 2)
    arrive(0, 0)
    arrive(1, 0)
    arrive(0, 1)
    arrive(1, 1)
    hop(0, 1, 3)
    hop(1, 1, 3)
    for k in (2, 3, 4):
        arrive(0, k)
        arrive(1, k)

    nt = (((1,), (1,)), ((), ()))

    def by_panel(a):
        return lax.dot_general(wd[a], x[a].reshape(128, D), nt, preferred_element_type=F32)

    def blocks(a):
        def one(c, _):
            xb[a, c] = x[a, :, :, pl.ds(mo(c * 128, 128), 128)].reshape(128, 128)
            return 0

        lax.fori_loop(0, NCOL, one, 0)

    def grads(dst, half):
        a = 1 - dst

        def one(i, _):
            s = i + half * (CAP // 2)
            pair = slot_pair[a, s]
            blk = jnp.dot(hd[dst, pair // NCOL], xb[a, pair % NCOL], preferred_element_type=F32)
            g[dst, pl.ds(mo(s * 128, 128), 128), :] = blk.astype(BF16)
            return 0

        lax.fori_loop(0, CAP // 2, one, 0, unroll=6)

    def partial(dst, side, a):
        acts = hd[side, :NPAN].reshape(512, 128).astype(F32).T.astype(BF16)

        def one(n, _):
            cols = pl.ds(mo(n * 512, 512), 512)
            part = jnp.dot(acts, wd[a, :, cols], preferred_element_type=F32)
            prt[dst, :, :, cols] = part.astype(BF16).reshape(NY, 16, 512)
            return 0

        lax.fori_loop(0, D // 512, one, 0)

    def scatter(a):
        nr, nl = rights[a], lefts[a]
        rc = [send(prt.at[a, (y + nr) % NY], rland.at[a, 0], right)]
        lc_ = [send(prt.at[a, (y + NY - nl) % NY], lland.at[a, 0], left)]
        for k in range(1, 4):
            for chain, land, n, to, sign in (
                (rc, rland, nr, right, 1),
                (lc_, lland, nl, left, NY - 1),
            ):
                if k >= n:
                    continue
                yield
                chain[k - 1].wait_recv()
                own = prt[a, (y + sign * (n - k)) % NY].astype(F32)
                land[a, k - 1] = (own + land[a, k - 1].astype(F32)).astype(BF16)
                chain.append(send(land.at[a, k - 1], land.at[a, k], to))
        yield
        rc[-1].wait_recv()
        lc_[-1].wait_recv()
        t2[a] = (
            prt[a, y].astype(F32)
            + rland[a, nr - 1].astype(F32)
            + lland[a, nl - 1].astype(F32)
        )
        for j in range(NZ):
            for k in range(4):
                t1[a, 4 * k : 4 * k + 4, :] = t2[a, 4 * j : 4 * j + 4, 1024 * k : 1024 * (k + 1)]
            zs[a, j] = t1[a].astype(BF16)
        out = [
            send(zs.at[a, d], zl.at[a, NZ - d], to) for d, to in zip((1, 2, 3), z_devs)
        ]
        yield
        for c in out:
            c.wait_recv()
        total = zs[a, 0].astype(F32)
        for d in (1, 2, 3):
            total = total + zl[a, d].astype(F32)
        t1[a] = total
        dst = (mixed_o, igrad_o)[a]
        for k in range(4):
            dst[:, 1024 * k : 1024 * (k + 1)] = t1[a, 4 * k : 4 * k + 4, :].astype(BF16)

    ha1, ha2 = ((px + 1) // 2) % 2, px // 2
    hb1, hb2 = px // 2, px % 2
    half_rows = CAP * 64
    n1, n2, n3, n4 = (half_rows // m for m in (2, 4, 8, 16))

    def rows(ref, r, n):
        return ref.at[pl.ds(mo(r), n)]

    def reduce(a, half):
        i = 2 * a + half
        ga, fo = g.at[a], (outg_o, ing_o)[a]
        base = half * half_rows + core * n1
        other = half * half_rows + n1 - core * n1
        ra1 = base + ha1 * n3
        sa1 = base + n3 - ha1 * n3
        ra2 = ra1 + ha2 * n4
        sa2 = ra1 + n4 - ha2 * n4
        rb1 = base + n2 + hb1 * n3
        sb1 = base + n2 + n3 - hb1 * n3
        rb2 = rb1 + hb2 * n4
        sb2 = rb1 + n4 - hb2 * n4
        rk = ra2 + zlo * (rb2 - ra2)
        rs = rb2 + zlo * (ra2 - rb2)

        def add(r, n, land):
            def one(c, _):
                at = pl.ds(mo(r + c * n4), n4)
                got = land[pl.ds(mo(c * n4), n4)].astype(F32)
                g[a, at] = (g[a, at].astype(F32) + got).astype(BF16)
                return 0

            lax.fori_loop(0, n // n4, one, 0)

        c0 = send(rows(ga, other, n1), lc.at[i], core_dev)
        yield
        c0.wait_recv()
        add(base, n1, lc.at[i])
        c1 = send(rows(ga, sa1, n3), l1.at[i, 0], xa_dev)
        c2 = send(rows(ga, sb1, n3), l1.at[i, 1], xb_dev)
        yield
        c1.wait_recv()
        add(ra1, n3, l1.at[i, 0])
        c3 = send(rows(ga, sa2, n4), l2.at[i, 0], xb_dev)
        c2.wait_recv()
        add(rb1, n3, l1.at[i, 1])
        c4 = send(rows(ga, sb2, n4), l2.at[i, 1], xa_dev)
        yield
        c3.wait_recv()
        add(ra2, n4, l2.at[i, 0])
        c4.wait_recv()
        add(rb2, n4, l2.at[i, 1])
        c5 = send(rows(ga, rs, n4), l3.at[i], zlo_dev)
        yield
        c5.wait_recv()
        fo[pl.ds(mo(rk), n4)] = (
            g[a, pl.ds(mo(rk), n4)].astype(F32) + l3[i].astype(F32)
        ).astype(BF16)
        c6 = send(rows(fo, rk, n4), rows(fo, rk, n4), zlo_dev)
        yield
        c6.wait_recv()
        c7 = send(rows(fo, ra2, n4), rows(fo, ra2, n4), xb_dev)
        c8 = send(rows(fo, rb2, n4), rows(fo, rb2, n4), xa_dev)
        yield
        c7.wait_recv()
        c9 = send(rows(fo, ra1, n3), rows(fo, ra1, n3), xa_dev)
        c8.wait_recv()
        c10 = send(rows(fo, rb1, n3), rows(fo, rb1, n3), xb_dev)
        yield
        c9.wait_recv()
        c10.wait_recv()
        c11 = send(rows(fo, base, n1), rows(fo, base, n1), core_dev)
        yield
        c11.wait_recv()

    def step(task):
        next(task, None)

    pre = by_panel(0)
    cdf = 0.5 * (1.0 + lax.erf(pre * 0.7071067811865476))
    hd[0, :NPAN] = (pre * cdf).astype(BF16).reshape(NPAN, 128, 128)
    slope = cdf + pre * jnp.exp(-0.5 * pre * pre) * 0.3989422804014327
    d_pre = lax.dot_general(
        wd[1], x[1].reshape(128, D), nt, preferred_element_type=F32
    )
    hd[1, :NPAN] = (d_pre * slope).astype(BF16).reshape(NPAN, 128, 128)

    red = [reduce(i // 2, i % 2) for i in range(4)]
    sc0, sc1 = scatter(0), scatter(1)
    blocks(1)
    grads(0, 0)
    step(red[0])
    grads(0, 1)
    step(red[1])
    blocks(0)
    step(red[0])
    grads(1, 0)
    step(red[2])
    step(red[1])
    grads(1, 1)
    step(red[3])
    step(red[0])
    partial(0, 0, 1)
    step(sc0)
    for i in (1, 2, 3, 0):
        step(red[i])
    partial(1, 1, 0)
    step(sc1)
    tasks = [red[1], red[2], sc0, red[3], red[0], sc1]
    while tasks:
        for task in list(tasks):
            if next(task, tasks) is tasks:
                tasks.remove(task)
    for c in started:
        c.wait_send()


def copy_out(*refs):
    n = (len(refs) - 1) // 2
    copies = [pltpu.make_async_copy(refs[i], refs[n + i], refs[-1].at[i]) for i in range(n)]
    for c in copies:
        c.start()
    for c in copies:
        c.wait()


def slot_tables(in_rows, in_cols, out_rows, out_cols):
    rows, cols = jnp.stack([in_rows, out_rows]), jnp.stack([in_cols, out_cols])
    pair = jnp.where(rows >= 0, (rows % NPAN) * NCOL + cols, NPAN * NCOL)
    slot = jnp.arange(CAP, dtype=jnp.int32)
    hit = pair[:, :, None] == jnp.arange(NPAN * NCOL, dtype=jnp.int32)[None, None, :]
    return pair, jnp.min(jnp.where(hit, slot[None, :, None], CAP), axis=1)


def local(tokens, cotangent, w_in, w_out, in_rows, in_cols, out_rows, out_cols):
    smem = pl.BlockSpec(memory_space=pltpu.SMEM)
    hbm = pl.BlockSpec(memory_space=pl.ANY)
    vmem = pl.BlockSpec(memory_space=pltpu.VMEM)
    rows = tokens.shape[0]
    shapes = [(rows, D), (rows, D), (CAP * 128, 128), (CAP * 128, 128)]
    slot_pair, pair_slot = slot_tables(in_rows, in_cols, out_rows, out_cols)
    half = CAP * 64
    results = pl.pallas_call(
        kernel,
        out_shape=tuple(pltpu.VMEM(s, BF16) for s in shapes),
        in_specs=[hbm, hbm, hbm, hbm, smem, smem],
        out_specs=(vmem,) * 4,
        scratch_shapes=[
            pltpu.VMEM((2, rows, D), BF16),
            pltpu.VMEM((2, NY, NZ, 16, 1024), BF16),
            pltpu.VMEM((2, NY, 16, D), BF16),
            pltpu.VMEM((2, 16, 1024), F32),
            pltpu.VMEM((2, 16, D), F32),
            pltpu.VMEM((2, CAP + 1, 128, 128), BF16),
            pltpu.VMEM((2, 512, D), BF16),
            pltpu.VMEM((2, NCOL, 128, 128), BF16),
            pltpu.VMEM((2, NPAN + 1, 128, 128), BF16),
            pltpu.VMEM((2, NY, 16, D), BF16),
            pltpu.VMEM((2, 4, 16, D), BF16),
            pltpu.VMEM((2, 4, 16, D), BF16),
            pltpu.VMEM((2, NZ, 16, 1024), BF16),
            pltpu.VMEM((2, NZ, 16, 1024), BF16),
            pltpu.VMEM((2, CAP * 128, 128), BF16),
            pltpu.VMEM((4, half // 2, 128), BF16),
            pltpu.VMEM((4, 2, half // 8, 128), BF16),
            pltpu.VMEM((4, 2, half // 16, 128), BF16),
            pltpu.VMEM((4, half // 16, 128), BF16),
            pltpu.SemaphoreType.DMA((SEMS,)),
            pltpu.SemaphoreType.DMA((SEMS,)),
            pltpu.SemaphoreType.DMA((4,)),
        ],
        compiler_params=pltpu.CompilerParams(
            collective_id=0, has_side_effects=True, vmem_limit_bytes=52 * 2**20
        ),
    )(tokens, cotangent, w_in, w_out, pair_slot, slot_pair)
    mixed, igrad, ing, outg = pl.pallas_call(
        copy_out,
        out_shape=tuple(jax.ShapeDtypeStruct(s, BF16) for s in shapes),
        in_specs=[vmem] * 4,
        out_specs=(hbm,) * 4,
        scratch_shapes=[pltpu.SemaphoreType.DMA((4,))],
        compiler_params=pltpu.CompilerParams(has_side_effects=True),
    )(*(pltpu.with_memory_space_constraint(r, pltpu.VMEM) for r in results))
    return mixed, igrad, ing.reshape(CAP, 128, 128), outg.reshape(CAP, 128, 128)


def solution(mesh):
    placed = (
        P(("dp", "fsdp"), None),
        P(("dp", "fsdp"), None),
        P("fsdp", None, None),
        P("fsdp", None, None),
        P("fsdp"),
        P("fsdp"),
        P("fsdp"),
        P("fsdp"),
    )
    return jax.shard_map(
        local,
        mesh=mesh,
        in_specs=placed,
        out_specs=(
            P(("dp", "fsdp"), None),
            P(("dp", "fsdp"), None),
            P("fsdp", None, None),
            P("fsdp", None, None),
        ),
        check_vma=False,
    )
```

time: 102 us -> 91.8 us (0.900)
  the two profiles are of different devices: /device:TPU:24 before, /device:TPU:8 now
where the time goes in v2:
time: 91.8 us; the launch traced here: 91.6 us
  Pallas kernels  89.5 us (97%)
  other arithmetic  1.4 us (2%)
    pallas_call x1, Pallas kernels, local(): pl.pallas_call(kernel, out_shape=tuple((pltpu.VMEM(s, BF16) for s in shap...  88 us

profile of v2, /device:TPU:8, one launch (start us, length us, event | category | flops | bytes accessed | tf_op | source)
XLA Modules:
  0.0 91.6 jit_solution(16156298381740995864)
XLA Ops:
  0.6 0.7 compare_select_fusion.3.slot_pair
  1.4 0.0 copy-start
  1.4 0.1 copy.12
  1.5 0.7 fusion.pair_slot
  2.1 0.0 copy-done
  2.1 88.0 %shard_map.111 = (bf16[4,4096]{1,0:T(4,128)(2,1)S(1)}, bf16[4,4096]{1,0:T(4,128)(2,1)S(1)}, bf16[4608,128]{1,0:T(8,128)(2,1)S(1)}, bf16[4608,128]{1,0:T(8,128)(2,1)S(1)}) custom-call(bf16[4,4096]{1,0:T(4,128)(2,1)} %tok.1, bf16[4,4096]{1,0:T(4,128)(2,1)} %cot.1, bf16[36,128,128]{2,1,0:T(8,128)(2,1)} %w_in.1, bf16[36,128,128]{2,1,0:T(8,128)(2,1)} %w_out.1, ...), custom_call_target="tpu_custom_call" | custom-call | tf_op jit(solution)/shard_map/pallas_call | solution.py:385
  90.2 1.5 %shard_map.112 = (bf16[4,4096]{1,0:T(4,128)(2,1)}, bf16[4,4096]{1,0:T(4,128)(2,1)}, bf16[4608,128]{1,0:T(8,128)(2,1)}, bf16[4608,128]{1,0:T(8,128)(2,1)}) custom-call(bf16[4,4096]{1,0:T(4,128)(2,1)S(1)} %get-tuple-element.12.refs_0_, bf16[4,4096]{1,0:T(4,128)(2,1)S(1)} %get-tuple-element.13.refs_1_, bf16[4608,128]{1,0:T(8,128)(2,1)S(1)} %get-tuple-element.14.refs_2_, ...), custom_call_target="tpu_custom_call" | custom-call | tf_op jit(solution)/shard_map/pallas_call | solution.py:418
Async XLA Ops:
  1.4 0.8 copy-start

commit v3 on v2

--- a/solution.py
+++ b/solution.py
@@ -24,7 +24,7 @@
 def kernel(
     tok, cot, w_in, w_out, pair_slot, slot_pair,
     mixed_o, igrad_o, ing_o, outg_o,
-    own, xg, x, t1, t2, ws, wd, xb, hd, prt, rland, lland, zs, zl, g, lc, l1, l2, l3,
+    own, xg, x, t1, t2, t3, t4, ws, wd, xb, hd, acts, prt, rland, lland, zs, zl, g, lc, l1, l2, l3, slope_ref,
     ssem, rsem, lsem,
 ):
     dp, fs = lax.axis_index("dp"), lax.axis_index("fsdp")
@@ -95,7 +95,10 @@
             t1[a] = xg[a, b, d].astype(F32)
             for k in range(4):
                 t2[a, 4 * d : 4 * d + 4, 1024 * k : 1024 * (k + 1)] = t1[a, 4 * k : 4 * k + 4, :]
-        x[a, b] = t2[a].astype(BF16)
+        rows = t2[a].astype(BF16)
+        x[a, b] = rows
+        for c in range(NCOL):
+            xb[a, c, pl.ds(mo(b * 16), 16), :] = rows[:, 128 * c : 128 * (c + 1)]
 
     rights, lefts = (4, 3), (3, 4)
     chains = {}
@@ -158,23 +161,17 @@
     arrive(1, 0)
     arrive(0, 1)
     arrive(1, 1)
+    arrive(0, 2)
+    arrive(1, 2)
     hop(0, 1, 3)
     hop(1, 1, 3)
-    for k in (2, 3, 4):
-        arrive(0, k)
-        arrive(1, k)
+    arrive(0, 3)
+    arrive(0, 4)
 
     nt = (((1,), (1,)), ((), ()))
 
     def by_panel(a):
         return lax.dot_general(wd[a], x[a].reshape(128, D), nt, preferred_element_type=F32)
-
-    def blocks(a):
-        def one(c, _):
-            xb[a, c] = x[a, :, :, pl.ds(mo(c * 128, 128), 128)].reshape(128, 128)
-            return 0
-
-        lax.fori_loop(0, NCOL, one, 0)
 
     def grads(dst, half):
         a = 1 - dst
@@ -188,58 +185,63 @@
 
         lax.fori_loop(0, CAP // 2, one, 0, unroll=6)
 
-    def partial(dst, side, a):
-        acts = hd[side, :NPAN].reshape(512, 128).astype(F32).T.astype(BF16)
-
+    half_d = D // 2
+
+    def by_token(side):
+        acts[side] = hd[side, :NPAN].reshape(512, 128).astype(F32).T.astype(BF16)
+
+    def partial(a, half):
         def one(n, _):
-            cols = pl.ds(mo(n * 512, 512), 512)
-            part = jnp.dot(acts, wd[a, :, cols], preferred_element_type=F32)
-            prt[dst, :, :, cols] = part.astype(BF16).reshape(NY, 16, 512)
+            cols = pl.ds(mo(half * half_d + n * 512, 512), 512)
+            part = jnp.dot(acts[a], wd[1 - a, :, cols], preferred_element_type=F32)
+            prt[a, half, :, :, pl.ds(mo(n * 512, 512), 512)] = part.astype(BF16).reshape(NY, 16, 512)
             return 0
 
-        lax.fori_loop(0, D // 512, one, 0)
-
-    def scatter(a):
-        nr, nl = rights[a], lefts[a]
-        rc = [send(prt.at[a, (y + nr) % NY], rland.at[a, 0], right)]
-        lc_ = [send(prt.at[a, (y + NY - nl) % NY], lland.at[a, 0], left)]
+        lax.fori_loop(0, half_d // 512, one, 0)
+
+    def scatter(a, half):
+        own_part, from_left, from_right = prt.at[a, half], rland.at[a, half], lland.at[a, half]
+        send_z, land_z = zs.at[a, half], zl.at[a, half]
+        nr, nl = rights[a ^ half], lefts[a ^ half]
+        ways = (
+            ([send(own_part.at[(y + nr) % NY], from_left.at[0], right)], from_left, nr, right, 1),
+            ([send(own_part.at[(y + NY - nl) % NY], from_right.at[0], left)], from_right, nl, left, NY - 1),
+        )
         for k in range(1, 4):
-            for chain, land, n, to, sign in (
-                (rc, rland, nr, right, 1),
-                (lc_, lland, nl, left, NY - 1),
-            ):
-                if k >= n:
-                    continue
-                yield
-                chain[k - 1].wait_recv()
-                own = prt[a, (y + sign * (n - k)) % NY].astype(F32)
-                land[a, k - 1] = (own + land[a, k - 1].astype(F32)).astype(BF16)
-                chain.append(send(land.at[a, k - 1], land.at[a, k], to))
-        yield
-        rc[-1].wait_recv()
-        lc_[-1].wait_recv()
-        t2[a] = (
-            prt[a, y].astype(F32)
-            + rland[a, nr - 1].astype(F32)
-            + lland[a, nl - 1].astype(F32)
+            yield
+            for chain, land, n, to, sign in ways:
+                if k < n:
+                    chain[k - 1].wait_recv()
+                    mine = own_part[(y + sign * (n - k)) % NY].astype(F32)
+                    land[k - 1] = (mine + land[k - 1].astype(F32)).astype(BF16)
+                    chain.append(send(land.at[k - 1], land.at[k], to))
+        yield
+        for chain, _, _, _, _ in ways:
+            chain[-1].wait_recv()
+        t3[...] = (
+            own_part[y].astype(F32)
+            + from_left[nr - 1].astype(F32)
+            + from_right[nl - 1].astype(F32)
         )
-        for j in range(NZ):
+        w = half_d // 4
+        for d in range(NZ):
             for k in range(4):
-                t1[a, 4 * k : 4 * k + 4, :] = t2[a, 4 * j : 4 * j + 4, 1024 * k : 1024 * (k + 1)]
-            zs[a, j] = t1[a].astype(BF16)
+                t4[d, 4 * k : 4 * k + 4, :] = t3[4 * d : 4 * d + 4, w * k : w * (k + 1)]
+            send_z[d] = t4[d].astype(BF16)
         out = [
-            send(zs.at[a, d], zl.at[a, NZ - d], to) for d, to in zip((1, 2, 3), z_devs)
+            send(send_z.at[d], land_z.at[NZ - d], to) for d, to in zip((1, 2, 3), z_devs)
         ]
         yield
         for c in out:
             c.wait_recv()
-        total = zs[a, 0].astype(F32)
+        total = send_z[0].astype(F32)
         for d in (1, 2, 3):
-            total = total + zl[a, d].astype(F32)
-        t1[a] = total
+            total = total + land_z[d].astype(F32)
+        t4[0] = total
         dst = (mixed_o, igrad_o)[a]
         for k in range(4):
-            dst[:, 1024 * k : 1024 * (k + 1)] = t1[a, 4 * k : 4 * k + 4, :].astype(BF16)
+            at = half * half_d + w * k
+            dst[:, at : at + w] = t4[0, 4 * k : 4 * k + 4, :].astype(BF16)
 
     ha1, ha2 = ((px + 1) // 2) % 2, px // 2
     hb1, hb2 = px // 2, px % 2
@@ -262,8 +264,6 @@
         sb1 = base + n2 + n3 - hb1 * n3
         rb2 = rb1 + hb2 * n4
         sb2 = rb1 + n4 - hb2 * n4
-        rk = ra2 + zlo * (rb2 - ra2)
-        rs = rb2 + zlo * (ra2 - rb2)
 
         def add(r, n, land):
             def one(c, _):
@@ -292,15 +292,13 @@
         add(ra2, n4, l2.at[i, 0])
         c4.wait_recv()
         add(rb2, n4, l2.at[i, 1])
-        c5 = send(rows(ga, rs, n4), l3.at[i], zlo_dev)
-        yield
-        c5.wait_recv()
-        fo[pl.ds(mo(rk), n4)] = (
-            g[a, pl.ds(mo(rk), n4)].astype(F32) + l3[i].astype(F32)
-        ).astype(BF16)
-        c6 = send(rows(fo, rk, n4), rows(fo, rk, n4), zlo_dev)
-        yield
-        c6.wait_recv()
+        c5 = send(rows(ga, ra2, n4), l3.at[i, 0], zlo_dev)
+        c6 = send(rows(ga, rb2, n4), l3.at[i, 1], zlo_dev)
+        yield
+        for c, r, land in ((c5, ra2, l3.at[i, 0]), (c6, rb2, l3.at[i, 1])):
+            c.wait_recv()
+            both = g[a, pl.ds(mo(r), n4)].astype(F32) + land[...].astype(F32)
+            fo[pl.ds(mo(r), n4)] = both.astype(BF16)
         c7 = send(rows(fo, ra2, n4), rows(fo, ra2, n4), xb_dev)
         c8 = send(rows(fo, rb2, n4), rows(fo, rb2, n4), xa_dev)
         yield
@@ -318,37 +316,45 @@
     def step(task):
         next(task, None)
 
+    red = [reduce(i // 2, i % 2) for i in range(4)]
+    sca = [[scatter(a, half) for half in range(2)] for a in range(2)]
+
     pre = by_panel(0)
     cdf = 0.5 * (1.0 + lax.erf(pre * 0.7071067811865476))
     hd[0, :NPAN] = (pre * cdf).astype(BF16).reshape(NPAN, 128, 128)
-    slope = cdf + pre * jnp.exp(-0.5 * pre * pre) * 0.3989422804014327
-    d_pre = lax.dot_general(
-        wd[1], x[1].reshape(128, D), nt, preferred_element_type=F32
-    )
-    hd[1, :NPAN] = (d_pre * slope).astype(BF16).reshape(NPAN, 128, 128)
-
-    red = [reduce(i // 2, i % 2) for i in range(4)]
-    sc0, sc1 = scatter(0), scatter(1)
-    blocks(1)
+    slope_ref[...] = cdf + pre * jnp.exp(-0.5 * pre * pre) * 0.3989422804014327
+    by_token(0)
+    for half in range(2):
+        partial(0, half)
+        step(sca[0][half])
+    arrive(1, 3)
+    arrive(1, 4)
     grads(0, 0)
     step(red[0])
     grads(0, 1)
     step(red[1])
-    blocks(0)
+    step(sca[0][0])
+    d_pre = by_panel(1)
+    hd[1, :NPAN] = (d_pre * slope_ref[...]).astype(BF16).reshape(NPAN, 128, 128)
     step(red[0])
+    step(sca[0][1])
     grads(1, 0)
     step(red[2])
     step(red[1])
     grads(1, 1)
     step(red[3])
+    by_token(1)
     step(red[0])
-    partial(0, 0, 1)
-    step(sc0)
-    for i in (1, 2, 3, 0):
-        step(red[i])
-    partial(1, 1, 0)
-    step(sc1)
-    tasks = [red[1], red[2], sc0, red[3], red[0], sc1]
+    partial(1, 0)
+    step(sca[1][0])
+    step(sca[0][0])
+    step(red[2])
+    partial(1, 1)
+    step(sca[1][1])
+    step(sca[0][1])
+    step(red[1])
+    step(red[3])
+    tasks = [red[0], sca[1][0], red[2], sca[0][0], red[1], sca[1][1], red[3], sca[0][1]]
     while tasks:
         for task in list(tasks):
             if next(task, tasks) is tasks:
@@ -393,20 +399,24 @@
             pltpu.VMEM((2, NY, 16, D), BF16),
             pltpu.VMEM((2, 16, 1024), F32),
             pltpu.VMEM((2, 16, D), F32),
+            pltpu.VMEM((16, D // 2), F32),
+            pltpu.VMEM((NZ, 16, D // 8), F32),
             pltpu.VMEM((2, CAP + 1, 128, 128), BF16),
             pltpu.VMEM((2, 512, D), BF16),
             pltpu.VMEM((2, NCOL, 128, 128), BF16),
             pltpu.VMEM((2, NPAN + 1, 128, 128), BF16),
-            pltpu.VMEM((2, NY, 16, D), BF16),
-            pltpu.VMEM((2, 4, 16, D), BF16),
-            pltpu.VMEM((2, 4, 16, D), BF16),
-            pltpu.VMEM((2, NZ, 16, 1024), BF16),
-            pltpu.VMEM((2, NZ, 16, 1024), BF16),
+            pltpu.VMEM((2, 128, 512), BF16),
+            pltpu.VMEM((2, 2, NY, 16, D // 2), BF16),
+            pltpu.VMEM((2, 2, 4, 16, D // 2), BF16),
+            pltpu.VMEM((2, 2, 4, 16, D // 2), BF16),
+            pltpu.VMEM((2, 2, NZ, 16, D // 8), BF16),
+            pltpu.VMEM((2, 2, NZ, 16, D // 8), BF16),
             pltpu.VMEM((2, CAP * 128, 128), BF16),
             pltpu.VMEM((4, half // 2, 128), BF16),
             pltpu.VMEM((4, 2, half // 8, 128), BF16),
             pltpu.VMEM((4, 2, half // 16, 128), BF16),
-            pltpu.VMEM((4, half // 16, 128), BF16),
+            pltpu.VMEM((4, 2, half // 16, 128), BF16),
+            pltpu.VMEM((512, 128), F32),
             pltpu.SemaphoreType.DMA((SEMS,)),
             pltpu.SemaphoreType.DMA((SEMS,)),
             pltpu.SemaphoreType.DMA((4,)),

time: 91.8 us -> 85.9 us (0.936)
  the two profiles are of different devices: /device:TPU:8 before, /device:TPU:1 now
where the time goes in v3:
time: 85.9 us; the launch traced here: 85.7 us
  Pallas kernels  83.6 us (97%)
  other arithmetic  1.4 us (2%)
    pallas_call x1, Pallas kernels, local(): pl.pallas_call(kernel, out_shape=tuple((pltpu.VMEM(s, BF16) for s in shap...  82.1 us

profile of v3, /device:TPU:1, one launch (start us, length us, event | category | flops | bytes accessed | tf_op | source)
XLA Modules:
  0.0 85.7 jit_solution(2976677576726513872)
XLA Ops:
  0.6 0.7 compare_select_fusion.3.slot_pair
  1.4 0.0 copy-start
  1.4 0.1 copy.12
  1.5 0.7 fusion.pair_slot
  2.1 0.0 copy-done
  2.1 82.1 %shard_map.111 = (bf16[4,4096]{1,0:T(4,128)(2,1)S(1)}, bf16[4,4096]{1,0:T(4,128)(2,1)S(1)}, bf16[4608,128]{1,0:T(8,128)(2,1)S(1)}, bf16[4608,128]{1,0:T(8,128)(2,1)S(1)}) custom-call(bf16[4,4096]{1,0:T(4,128)(2,1)} %tok.1, bf16[4,4096]{1,0:T(4,128)(2,1)} %cot.1, bf16[36,128,128]{2,1,0:T(8,128)(2,1)} %w_in.1, bf16[36,128,128]{2,1,0:T(8,128)(2,1)} %w_out.1, ...), custom_call_target="tpu_custom_call" | custom-call | tf_op jit(solution)/shard_map/pallas_call | solution.py:391
  84.2 1.5 %shard_map.112 = (bf16[4,4096]{1,0:T(4,128)(2,1)}, bf16[4,4096]{1,0:T(4,128)(2,1)}, bf16[4608,128]{1,0:T(8,128)(2,1)}, bf16[4608,128]{1,0:T(8,128)(2,1)}) custom-call(bf16[4,4096]{1,0:T(4,128)(2,1)S(1)} %get-tuple-element.12.refs_0_, bf16[4,4096]{1,0:T(4,128)(2,1)S(1)} %get-tuple-element.13.refs_1_, bf16[4608,128]{1,0:T(8,128)(2,1)S(1)} %get-tuple-element.14.refs_2_, ...), custom_call_target="tpu_custom_call" | custom-call | tf_op jit(solution)/shard_map/pallas_call | solution.py:428
Async XLA Ops:
  1.4 0.8 copy-start

commit v4 on v3

--- a/solution.py
+++ b/solution.py
@@ -14,7 +14,7 @@
 NCOL = 32
 NPAN = 4
 D = 4096
-SEMS = 128
+SEMS = 136
 
 
 def mo(v, m=16):
@@ -34,8 +34,8 @@
     def dev(d=dp, f=fs):
         return (d, f)
 
-    z_peers = [(zh + d) % NZ for d in (1, 2, 3)]
-    z_devs = [dev(f=y * NZ + j) for j in z_peers]
+    up, down, across = (dev(f=y * NZ + (zh + d) % NZ) for d in (1, 3, 2))
+    z_routes = ((1, up, 2), (2, down, 1), (3, across, 3))
     right = dev(f=((y + 1) % NY) * NZ + zh)
     left = dev(f=((y + NY - 1) % NY) * NZ + zh)
     core_dev = dev(d=dp + 1 - 2 * core)
@@ -44,7 +44,7 @@
     xa_dev = dev(d=xpa * 4 + dp % 4)
     xb_dev = dev(d=xpb * 4 + dp % 4)
     zlo_dev = dev(d=dp + 2 - 4 * zlo)
-    everyone = [*z_devs, right, left, core_dev, xa_dev, xb_dev, zlo_dev]
+    everyone = [up, down, across, right, left, core_dev, xa_dev, xb_dev, zlo_dev]
 
     used = [0]
     started = []
@@ -52,6 +52,7 @@
     def send(src, dst, to):
         i = used[0]
         used[0] += 1
+        assert i < SEMS
         c = pltpu.make_async_remote_copy(
             src, dst, ssem.at[i], rsem.at[i], device_id=to, device_id_type=MESH
         )
@@ -83,7 +84,7 @@
     pl.semaphore_wait(barrier, len(everyone))
 
     zsend = [
-        [send(xg.at[a, y, 0], xg.at[a, y, NZ - d], to) for d, to in zip((1, 2, 3), z_devs)]
+        [send(xg.at[a, y, 0], xg.at[a, y, there], to) for _, to, there in z_routes[:2]]
         for a in range(2)
     ]
     for a in range(2):
@@ -100,24 +101,36 @@
         for c in range(NCOL):
             xb[a, c, pl.ds(mo(b * 16), 16), :] = rows[:, 128 * c : 128 * (c + 1)]
 
+    groups = (pl.ds(0, 1), pl.ds(1, 2), pl.ds(3, 1))
     rights, lefts = (4, 3), (3, 4)
     chains = {}
 
-    def hop(a, grp, k):
-        part = (pl.ds(0, 1), pl.ds(1, 3))[grp]
-        for way, to, n, back in (
-            (0, right, rights[a ^ grp], NY - 1),
-            (1, left, lefts[a ^ grp], 1),
-        ):
-            chain = chains.setdefault((a, grp, way), [])
-            if k < n:
-                if k:
-                    chain[k - 1].wait_recv()
-                ref = xg.at[a, (y + back * k) % NY, part]
-                chain.append(send(ref, ref, to))
+    def hop(grp, k, arrays=(0, 1)):
+        for a in arrays:
+            for way, to, n, back in (
+                (0, right, rights[(a + grp) % 2], NY - 1),
+                (1, left, lefts[(a + grp) % 2], 1),
+            ):
+                chain = chains.setdefault((a, grp, way), [])
+                if k < n:
+                    if k:
+                        chain[k - 1].wait_recv()
+                    ref = xg.at[a, (y + back * k) % NY, groups[grp]]
+                    chain.append(send(ref, ref, to))
+
+    def z_near(a):
+        for c in zsend[a]:
+            c.wait_recv()
+        here, to = ((1, down), (2, up))[a]
+        zsend[a].append(send(xg.at[a, y, here], xg.at[a, y, 3], to))
+        hop(1, 0, (a,))
+
+    def z_far(a):
+        zsend[a][2].wait_recv()
+        hop(2, 0, (a,))
 
     def arrive(a, k):
-        for grp in range(2):
+        for grp in range(3):
             for way in range(2):
                 chain = chains[(a, grp, way)]
                 if k == len(chain):
@@ -139,33 +152,30 @@
 
         lax.fori_loop(0, NCOL, one, 0)
 
-    hop(0, 0, 0)
-    hop(1, 0, 0)
-    hop(0, 0, 1)
-    hop(1, 0, 1)
-    for a in range(2):
-        for c in zsend[a]:
-            c.wait_recv()
-        hop(a, 1, 0)
-    hop(0, 0, 2)
-    hop(1, 0, 2)
+    hop(0, 0)
     dense(0)
-    hop(0, 1, 1)
-    hop(1, 1, 1)
-    hop(0, 0, 3)
-    hop(1, 0, 3)
+    hop(0, 1)
+    z_near(0)
+    z_near(1)
+    hop(0, 2)
+    z_far(0)
+    z_far(1)
+    hop(1, 1)
     dense(1)
-    hop(0, 1, 2)
-    hop(1, 1, 2)
+    hop(0, 3)
+    hop(2, 1)
+    hop(1, 2)
     arrive(0, 0)
     arrive(1, 0)
+    hop(2, 2)
     arrive(0, 1)
     arrive(1, 1)
+    hop(1, 3)
     arrive(0, 2)
+    hop(2, 3)
     arrive(1, 2)
-    hop(0, 1, 3)
-    hop(1, 1, 3)
     arrive(0, 3)
+    arrive(1, 3)
     arrive(0, 4)
 
     nt = (((1,), (1,)), ((), ()))
@@ -183,7 +193,7 @@
             g[dst, pl.ds(mo(s * 128, 128), 128), :] = blk.astype(BF16)
             return 0
 
-        lax.fori_loop(0, CAP // 2, one, 0, unroll=6)
+        lax.fori_loop(0, CAP // 2, one, 0, unroll=True)
 
     half_d = D // 2
 
@@ -191,13 +201,10 @@
         acts[side] = hd[side, :NPAN].reshape(512, 128).astype(F32).T.astype(BF16)
 
     def partial(a, half):
-        def one(n, _):
-            cols = pl.ds(mo(half * half_d + n * 512, 512), 512)
-            part = jnp.dot(acts[a], wd[1 - a, :, cols], preferred_element_type=F32)
-            prt[a, half, :, :, pl.ds(mo(n * 512, 512), 512)] = part.astype(BF16).reshape(NY, 16, 512)
-            return 0
-
-        lax.fori_loop(0, half_d // 512, one, 0)
+        for n in range(0, half_d, 512):
+            at = half * half_d + n
+            part = jnp.dot(acts[a], wd[1 - a, :, at : at + 512], preferred_element_type=F32)
+            prt[a, half, :, :, n : n + 512] = part.astype(BF16).reshape(NY, 16, 512)
 
     def scatter(a, half):
         own_part, from_left, from_right = prt.at[a, half], rland.at[a, half], lland.at[a, half]
@@ -229,7 +236,7 @@
                 t4[d, 4 * k : 4 * k + 4, :] = t3[4 * d : 4 * d + 4, w * k : w * (k + 1)]
             send_z[d] = t4[d].astype(BF16)
         out = [
-            send(send_z.at[d], land_z.at[NZ - d], to) for d, to in zip((1, 2, 3), z_devs)
+            send(send_z.at[here], land_z.at[there], to) for here, to, there in z_routes
         ]
         yield
         for c in out:
@@ -319,46 +326,84 @@
     red = [reduce(i // 2, i % 2) for i in range(4)]
     sca = [[scatter(a, half) for half in range(2)] for a in range(2)]
 
-    pre = by_panel(0)
-    cdf = 0.5 * (1.0 + lax.erf(pre * 0.7071067811865476))
-    hd[0, :NPAN] = (pre * cdf).astype(BF16).reshape(NPAN, 128, 128)
-    slope_ref[...] = cdf + pre * jnp.exp(-0.5 * pre * pre) * 0.3989422804014327
-    by_token(0)
-    for half in range(2):
-        partial(0, half)
-        step(sca[0][half])
-    arrive(1, 3)
+    def activate():
+        pre = by_panel(0)
+        cdf = 0.5 * (1.0 + lax.erf(pre * 0.7071067811865476))
+        hd[0, :NPAN] = (pre * cdf).astype(BF16).reshape(NPAN, 128, 128)
+        slope_ref[...] = cdf + pre * jnp.exp(-0.5 * pre * pre) * 0.3989422804014327
+        by_token(0)
+
+    def differentiate():
+        hd[1, :NPAN] = (by_panel(1) * slope_ref[...]).astype(BF16).reshape(NPAN, 128, 128)
+        by_token(1)
+
+    activate()
     arrive(1, 4)
     grads(0, 0)
     step(red[0])
     grads(0, 1)
     step(red[1])
+    differentiate()
+    partial(1, 0)
+    partial(1, 1)
+    step(red[0])
+    step(sca[1][1])
+    step(sca[1][0])
+    grads(1, 0)
+    grads(1, 1)
+    step(red[3])
+    step(red[1])
+    step(red[2])
+    partial(0, 1)
+    step(sca[0][1])
+    partial(0, 0)
+    step(red[3])
     step(sca[0][0])
-    d_pre = by_panel(1)
-    hd[1, :NPAN] = (d_pre * slope_ref[...]).astype(BF16).reshape(NPAN, 128, 128)
-    step(red[0])
+    step(red[0])
+    step(sca[1][1])
+    step(red[2])
+    step(sca[1][0])
+    step(red[1])
     step(sca[0][1])
-    grads(1, 0)
-    step(red[2])
-    step(red[1])
-    grads(1, 1)
-    step(red[3])
-    by_token(1)
-    step(red[0])
-    partial(1, 0)
+    step(red[3])
+    step(sca[0][0])
+    step(red[0])
+    step(sca[1][1])
+    step(red[2])
+    step(red[1])
     step(sca[1][0])
+    step(red[3])
+    step(sca[0][1])
+    step(red[0])
+    step(red[2])
     step(sca[0][0])
-    step(red[2])
-    partial(1, 1)
+    step(red[1])
     step(sca[1][1])
+    step(red[0])
+    step(red[3])
+    step(sca[1][0])
     step(sca[0][1])
-    step(red[1])
-    step(red[3])
-    tasks = [red[0], sca[1][0], red[2], sca[0][0], red[1], sca[1][1], red[3], sca[0][1]]
-    while tasks:
-        for task in list(tasks):
-            if next(task, tasks) is tasks:
-                tasks.remove(task)
+    step(red[2])
+    step(red[1])
+    step(sca[0][0])
+    step(red[0])
+    step(sca[1][1])
+    step(red[3])
+    step(sca[1][0])
+    step(red[2])
+    step(sca[0][1])
+    step(sca[0][0])
+    step(red[1])
+    step(red[0])
+    step(red[3])
+    step(sca[1][1])
+    step(red[1])
+    step(sca[1][0])
+    step(red[2])
+    step(red[3])
+    step(sca[0][1])
+    step(sca[0][0])
+    step(red[2])
     for c in started:
         c.wait_send()
 
@@ -378,6 +423,10 @@
     slot = jnp.arange(CAP, dtype=jnp.int32)
     hit = pair[:, :, None] == jnp.arange(NPAN * NCOL, dtype=jnp.int32)[None, None, :]
     return pair, jnp.min(jnp.where(hit, slot[None, :, None], CAP), axis=1)
+
+
+def near(value):
+    return pltpu.with_memory_space_constraint(value, pltpu.VMEM)
 
 
 def local(tokens, cotangent, w_in, w_out, in_rows, in_cols, out_rows, out_cols):
@@ -432,7 +481,7 @@
         out_specs=(hbm,) * 4,
         scratch_shapes=[pltpu.SemaphoreType.DMA((4,))],
         compiler_params=pltpu.CompilerParams(has_side_effects=True),
-    )(*(pltpu.with_memory_space_constraint(r, pltpu.VMEM) for r in results))
+    )(*map(near, results))
     return mixed, igrad, ing.reshape(CAP, 128, 128), outg.reshape(CAP, 128, 128)
 
 

time: 85.9 us -> 80.3 us (0.935)
  Pallas kernels: 83.6 us -> 78 us
    pallas_call x1, Pallas kernels: 82.1 us -> 76.5 us  [local(): pl.pallas_call(kernel, out_shape=tuple((pltpu.VMEM(s, BF16) for s in shap...]
where the time goes in v4:
time: 80.3 us; the launch traced here: 80.1 us
  Pallas kernels  78 us (97%)
  other arithmetic  1.4 us (2%)
    pallas_call x1, Pallas kernels, local(): pl.pallas_call(kernel, out_shape=tuple((pltpu.VMEM(s, BF16) for s in shap...  76.5 us

profile of v4, /device:TPU:1, one launch (start us, length us, event | category | flops | bytes accessed | tf_op | source)
XLA Modules:
  0.0 80.1 jit_solution(18156891634160048268)
XLA Ops:
  0.6 0.7 compare_select_fusion.3.slot_pair
  1.4 0.0 copy-start
  1.4 0.1 copy.12
  1.5 0.7 fusion.pair_slot
  2.1 0.0 copy-done
  2.1 76.5 %shard_map.111 = (bf16[4,4096]{1,0:T(4,128)(2,1)S(1)}, bf16[4,4096]{1,0:T(4,128)(2,1)S(1)}, bf16[4608,128]{1,0:T(8,128)(2,1)S(1)}, bf16[4608,128]{1,0:T(8,128)(2,1)S(1)}) custom-call(bf16[4,4096]{1,0:T(4,128)(2,1)} %tok.1, bf16[4,4096]{1,0:T(4,128)(2,1)} %cot.1, bf16[36,128,128]{2,1,0:T(8,128)(2,1)} %w_in.1, bf16[36,128,128]{2,1,0:T(8,128)(2,1)} %w_out.1, ...), custom_call_target="tpu_custom_call" | custom-call | tf_op jit(solution)/shard_map/pallas_call | solution.py:440
  78.7 1.5 %shard_map.112 = (bf16[4,4096]{1,0:T(4,128)(2,1)}, bf16[4,4096]{1,0:T(4,128)(2,1)}, bf16[4608,128]{1,0:T(8,128)(2,1)}, bf16[4608,128]{1,0:T(8,128)(2,1)}) custom-call(bf16[4,4096]{1,0:T(4,128)(2,1)S(1)} %get-tuple-element.12.refs_0_, bf16[4,4096]{1,0:T(4,128)(2,1)S(1)} %get-tuple-element.13.refs_1_, bf16[4608,128]{1,0:T(8,128)(2,1)S(1)} %get-tuple-element.14.refs_2_, ...), custom_call_target="tpu_custom_call" | custom-call | tf_op jit(solution)/shard_map/pallas_call | solution.py:477
Async XLA Ops:
  1.4 0.8 copy-start

commit v5 on v4

--- a/solution.py
+++ b/solution.py
@@ -22,9 +22,9 @@
 
 
 def kernel(
-    tok, cot, w_in, w_out, pair_slot, slot_pair,
+    tok, cot, w_in, w_out, in_rows, in_cols, out_rows, out_cols,
     mixed_o, igrad_o, ing_o, outg_o,
-    own, xg, x, t1, t2, t3, t4, ws, wd, xb, hd, acts, prt, rland, lland, zs, zl, g, lc, l1, l2, l3, slope_ref,
+    own, xg, x, t1, t2, t3, t4, ws, wd, xb, hd, acts, prt, rland, lland, zs, zl, g, lc, l1, l2, l3, slope_ref, table, pair_slot,
     ssem, rsem, lsem,
 ):
     dp, fs = lax.axis_index("dp"), lax.axis_index("fsdp")
@@ -60,10 +60,6 @@
         started.append(c)
         return c
 
-    barrier = pltpu.get_barrier_semaphore()
-    for to in everyone:
-        pl.semaphore_signal(barrier, inc=1, device_id=to, device_id_type=MESH)
-
     fetch = [
         pltpu.make_async_copy(src, own.at[a], lsem.at[2 + a])
         for a, src in enumerate((tok, cot))
@@ -72,7 +68,13 @@
         pltpu.make_async_copy(w, ws.at[a, pl.ds(0, CAP)], lsem.at[a])
         for a, w in enumerate((w_in, w_out))
     ]
-    for c in fetch + weights:
+    for c in fetch:
+        c.start()
+
+    barrier = pltpu.get_barrier_semaphore()
+    for to in everyone:
+        pl.semaphore_signal(barrier, inc=1, device_id=to, device_id_type=MESH)
+    for c in weights:
         c.start()
 
     for a in range(2):
@@ -146,13 +148,26 @@
 
         def one(c, _):
             for p in range(NPAN):
-                slot = pair_slot[a, p * NCOL + c]
+                slot = pair_slot[a, 0, p * NCOL + c]
                 wd[a, pl.ds(p * 128, 128), pl.ds(mo(c * 128, 128), 128)] = ws[a, slot]
             return 0
 
         lax.fori_loop(0, NCOL, one, 0)
 
     hop(0, 0)
+
+    lane = lax.broadcasted_iota(jnp.int32, (8, 128), 1)
+    for a, (rows, cols) in enumerate(((in_rows, in_cols), (out_rows, out_cols))):
+
+        def find(s, found, rows=rows, cols=cols):
+            live = (rows[s] + 128) // 128
+            code = live * (rows[s] % NPAN * NCOL + cols[s]) + (1 - live) * (NPAN * NCOL)
+            return jnp.where(lane == code, s, found)
+
+        table[a] = lax.fori_loop(0, CAP, find, jnp.full((8, 128), CAP, jnp.int32))
+    to_scalars = pltpu.make_async_copy(table, pair_slot, lsem.at[4])
+    to_scalars.start()
+    to_scalars.wait()
     dense(0)
     hop(0, 1)
     z_near(0)
@@ -185,11 +200,13 @@
 
     def grads(dst, half):
         a = 1 - dst
+        rows, cols = ((out_rows, out_cols), (in_rows, in_cols))[dst]
 
         def one(i, _):
             s = i + half * (CAP // 2)
-            pair = slot_pair[a, s]
-            blk = jnp.dot(hd[dst, pair // NCOL], xb[a, pair % NCOL], preferred_element_type=F32)
+            live = (rows[s] + 128) // 128
+            panel = NPAN - live * (NPAN - rows[s] % NPAN)
+            blk = jnp.dot(hd[dst, panel], xb[a, live * cols[s]], preferred_element_type=F32)
             g[dst, pl.ds(mo(s * 128, 128), 128), :] = blk.astype(BF16)
             return 0
 
@@ -417,14 +434,6 @@
         c.wait()
 
 
-def slot_tables(in_rows, in_cols, out_rows, out_cols):
-    rows, cols = jnp.stack([in_rows, out_rows]), jnp.stack([in_cols, out_cols])
-    pair = jnp.where(rows >= 0, (rows % NPAN) * NCOL + cols, NPAN * NCOL)
-    slot = jnp.arange(CAP, dtype=jnp.int32)
-    hit = pair[:, :, None] == jnp.arange(NPAN * NCOL, dtype=jnp.int32)[None, None, :]
-    return pair, jnp.min(jnp.where(hit, slot[None, :, None], CAP), axis=1)
-
-
 def near(value):
     return pltpu.with_memory_space_constraint(value, pltpu.VMEM)
 
@@ -435,12 +444,11 @@
     vmem = pl.BlockSpec(memory_space=pltpu.VMEM)
     rows = tokens.shape[0]
     shapes = [(rows, D), (rows, D), (CAP * 128, 128), (CAP * 128, 128)]
-    slot_pair, pair_slot = slot_tables(in_rows, in_cols, out_rows, out_cols)
     half = CAP * 64
     results = pl.pallas_call(
         kernel,
         out_shape=tuple(pltpu.VMEM(s, BF16) for s in shapes),
-        in_specs=[hbm, hbm, hbm, hbm, smem, smem],
+        in_specs=[hbm] * 4 + [smem] * 4,
         out_specs=(vmem,) * 4,
         scratch_shapes=[
             pltpu.VMEM((2, rows, D), BF16),
@@ -466,14 +474,16 @@
             pltpu.VMEM((4, 2, half // 16, 128), BF16),
             pltpu.VMEM((4, 2, half // 16, 128), BF16),
             pltpu.VMEM((512, 128), F32),
+            pltpu.VMEM((2, 8, 128), jnp.int32),
+            pltpu.SMEM((2, 8, 128), jnp.int32),
             pltpu.SemaphoreType.DMA((SEMS,)),
             pltpu.SemaphoreType.DMA((SEMS,)),
-            pltpu.SemaphoreType.DMA((4,)),
+            pltpu.SemaphoreType.DMA((5,)),
         ],
         compiler_params=pltpu.CompilerParams(
             collective_id=0, has_side_effects=True, vmem_limit_bytes=52 * 2**20
         ),
-    )(tokens, cotangent, w_in, w_out, pair_slot, slot_pair)
+    )(tokens, cotangent, w_in, w_out, in_rows, in_cols, out_rows, out_cols)
     mixed, igrad, ing, outg = pl.pallas_call(
         copy_out,
         out_shape=tuple(jax.ShapeDtypeStruct(s, BF16) for s in shapes),

time: 80.3 us -> 78.9 us (0.983)
  other arithmetic: 1.4 us -> 0 us
where the time goes in v5:
time: 78.9 us; the launch traced here: 78.7 us
  Pallas kernels  78.1 us (99%)
    pallas_call x1, Pallas kernels, local(): pl.pallas_call(kernel, out_shape=tuple((pltpu.VMEM(s, BF16) for s in shap...  76.6 us

profile of v5, /device:TPU:1, one launch (start us, length us, event | category | flops | bytes accessed | tf_op | source)
XLA Modules:
  0.0 78.7 jit_solution(17969958058208147500)
XLA Ops:
  0.6 76.6 %shard_map.111 = (bf16[4,4096]{1,0:T(4,128)(2,1)S(1)}, bf16[4,4096]{1,0:T(4,128)(2,1)S(1)}, bf16[4608,128]{1,0:T(8,128)(2,1)S(1)}, bf16[4608,128]{1,0:T(8,128)(2,1)S(1)}) custom-call(bf16[4,4096]{1,0:T(4,128)(2,1)} %tok.1, bf16[4,4096]{1,0:T(4,128)(2,1)} %cot.1, bf16[36,128,128]{2,1,0:T(8,128)(2,1)} %w_in.1, bf16[36,128,128]{2,1,0:T(8,128)(2,1)} %w_out.1, ...), custom_call_target="tpu_custom_call" | custom-call | tf_op jit(solution)/shard_map/pallas_call | solution.py:448
  77.3 1.5 %shard_map.112 = (bf16[4,4096]{1,0:T(4,128)(2,1)}, bf16[4,4096]{1,0:T(4,128)(2,1)}, bf16[4608,128]{1,0:T(8,128)(2,1)}, bf16[4608,128]{1,0:T(8,128)(2,1)}) custom-call(bf16[4,4096]{1,0:T(4,128)(2,1)S(1)} %get-tuple-element.12.refs_0_, bf16[4,4096]{1,0:T(4,128)(2,1)S(1)} %get-tuple-element.13.refs_1_, bf16[4608,128]{1,0:T(8,128)(2,1)S(1)} %get-tuple-element.14.refs_2_, ...), custom_call_target="tpu_custom_call" | custom-call | tf_op jit(solution)/shard_map/pallas_call | solution.py:487

commit v6 on v5

--- a/solution.py
+++ b/solution.py
@@ -77,18 +77,19 @@
     for c in weights:
         c.start()
 
-    for a in range(2):
+    def fold_own(a):
         fetch[a].wait()
         for k in range(4):
             t1[a, 4 * k : 4 * k + 4, :] = own[a, :, 1024 * k : 1024 * (k + 1)].astype(F32)
         xg[a, y, 0] = t1[a].astype(BF16)
 
+    fold_own(0)
     pl.semaphore_wait(barrier, len(everyone))
-
-    zsend = [
-        [send(xg.at[a, y, 0], xg.at[a, y, there], to) for _, to, there in z_routes[:2]]
-        for a in range(2)
-    ]
+    zsend = []
+    for a in range(2):
+        if a:
+            fold_own(a)
+        zsend.append([send(xg.at[a, y, 0], xg.at[a, y, there], to) for _, to, there in z_routes[:2]])
     for a in range(2):
         ws[a, CAP] = jnp.zeros((128, 128), BF16)
         hd[a, NPAN] = jnp.zeros((128, 128), BF16)

time: 78.9 us -> 79 us (level)
  no operation moved by 1% of the time
where the time goes in v6:
time: 79 us; the launch traced here: 78.8 us
  Pallas kernels  78.2 us (99%)
    pallas_call x1, Pallas kernels, local(): pl.pallas_call(kernel, out_shape=tuple((pltpu.VMEM(s, BF16) for s in shap...  76.7 us

profile of v6, /device:TPU:1, one launch (start us, length us, event | category | flops | bytes accessed | tf_op | source)
XLA Modules:
  0.0 78.8 jit_solution(12309362977432995030)
XLA Ops:
  0.6 76.7 %shard_map.111 = (bf16[4,4096]{1,0:T(4,128)(2,1)S(1)}, bf16[4,4096]{1,0:T(4,128)(2,1)S(1)}, bf16[4608,128]{1,0:T(8,128)(2,1)S(1)}, bf16[4608,128]{1,0:T(8,128)(2,1)S(1)}) custom-call(bf16[4,4096]{1,0:T(4,128)(2,1)} %tok.1, bf16[4,4096]{1,0:T(4,128)(2,1)} %cot.1, bf16[36,128,128]{2,1,0:T(8,128)(2,1)} %w_in.1, bf16[36,128,128]{2,1,0:T(8,128)(2,1)} %w_out.1, ...), custom_call_target="tpu_custom_call" | custom-call | tf_op jit(solution)/shard_map/pallas_call | solution.py:449
  77.3 1.5 %shard_map.112 = (bf16[4,4096]{1,0:T(4,128)(2,1)}, bf16[4,4096]{1,0:T(4,128)(2,1)}, bf16[4608,128]{1,0:T(8,128)(2,1)}, bf16[4608,128]{1,0:T(8,128)(2,1)}) custom-call(bf16[4,4096]{1,0:T(4,128)(2,1)S(1)} %get-tuple-element.12.refs_0_, bf16[4,4096]{1,0:T(4,128)(2,1)S(1)} %get-tuple-element.13.refs_1_, bf16[4608,128]{1,0:T(8,128)(2,1)S(1)} %get-tuple-element.14.refs_2_, ...), custom_call_target="tpu_custom_call" | custom-call | tf_op jit(solution)/shard_map/pallas_call | solution.py:488
